TPU v7x, 512 devices: a whole 4x8x8 slice. The times are simulated.
512 devices in a mesh: section: 32 (over z, x), tensor: 16 (over y, core).
Axes of the slice: x: 4, y: 8, z: 8, core: 2. Of those that a mesh axis runs over, the one named last changes fastest.
Arguments:
- hidden_rows: bfloat16 [32, 2, 8192], P('section', None, 'tensor'), may hold values from -10 to 10
- entering_rows: bfloat16 [3, 2, 8192], P(None, None, 'tensor'), may hold values from -10 to 10
- norm_gain: bfloat16 [32, 8192], P('section', 'tensor'), may hold values from 0.099609375 to 1.8984375
- key_weight: bfloat16 [32, 8192, 512], P('section', 'tensor'), may hold values from -0.0625 to 0.0625
- value_weight: bfloat16 [32, 8192, 512], P('section', 'tensor'), may hold values from -0.0625 to 0.0625
- queries: bfloat16 [32, 4, 2, 8192], P('section'), may hold values from -8 to 8
- cache_keys: bfloat16 [32, 4, 2, 2048, 512], P('section', None, None, 'tensor'), may hold values from -50 to 50
- cache_values: bfloat16 [32, 4, 2, 2048, 512], P('section', None, None, 'tensor'), may hold values from -5 to 5
- lengths: int32 [4, 2], replicated, may hold values from 2 to 2048, as said below
- plan: int32 [4], replicated, may hold values from 0 to 3, each once
Outputs:
- processed_rows: bfloat16 [32, 2, 8192], P('section', None, 'tensor')
Inputs may be any that keep to these rules, and one draw needn't show every extreme that they name: `lengths`: every request has at least 2 cached positions, and in every draw some request has all 2048.
All inputs are finite; a program needn't handle non-finite values.
Results may differ from a plain program's by a relative error of at most 0.015.
Values may be sent and summed in bfloat16 or wider, within the bound.
A program may use at most 64 MiB of HBM per device.

v0:
```python
import jax
import jax.numpy as jnp
from jax import lax
from jax.sharding import PartitionSpec as P

D = 8192
HQ = 64
KVH = 4
HD = 128


epsilon = 1e-05
neg_big = -1e30


def merged(value, axis, combine):
    everything = jax.tree.map(
        lambda part, kind: lax.all_gather(part.astype(kind), axis),
        value,
        jax.tree.map(lambda a: jnp.bfloat16 if a.dtype == jnp.float32 else a.dtype, value),
    )

    def take(k):
        return jax.tree.map(lambda part, own: part[k].astype(own.dtype), everything, value)

    return lax.fori_loop(
        1, lax.axis_size(axis), lambda k, so_far: combine(so_far, take(k)), take(0)
    )


def from_behind(block, axis, distance):
    devices = range(lax.axis_size(axis))
    route = [(i - distance, i) for i in devices if i - distance in devices]
    return lax.ppermute(block, axis, route)


def rounded(values):
    return lax.optimization_barrier(values.astype(jnp.bfloat16)).astype(jnp.float32)


def rotate_keys(key_rows, position):
    half_dim = key_rows.shape[-1] // 2
    freq_rates = jnp.exp(
        jnp.arange(half_dim, dtype=jnp.float32) * (-2.0 * jnp.log(500000.0) / key_rows.shape[-1])
    )
    angle_row = position.astype(jnp.float32)[:, None] * freq_rates[None, :]
    cosine = jnp.cos(angle_row)[:, None, :]
    sine_part = jnp.sin(angle_row)[:, None, :]
    first_half = key_rows[..., :half_dim]
    second_half = key_rows[..., half_dim:]
    return jnp.concatenate(
        [
            first_half * cosine - second_half * sine_part,
            second_half * cosine + first_half * sine_part,
        ],
        axis=-1,
    )


def join_parts(first_part, second_part):
    row_top = jnp.maximum(first_part[0], second_part[0])
    weight_left = jnp.exp(first_part[0] - row_top)
    weight_right = jnp.exp(second_part[0] - row_top)
    row_total = first_part[1] * weight_left + second_part[1] * weight_right
    mixed_sum = first_part[2] * weight_left[..., None] + second_part[2] * weight_right[..., None]
    return (row_top, row_total, mixed_sum)


def cache_stats(query_rows, key_block, value_block, length, offset):
    req_count = query_rows.shape[0]
    positions = key_block.shape[1]
    group_size = HQ // KVH
    query_all = query_rows.reshape(req_count, KVH, group_size, HD)
    key_all = key_block.reshape(req_count, positions, KVH, HD)
    value_all = value_block.reshape(req_count, positions, KVH, HD)
    scores = jnp.einsum(
        "rkgd,rpkd->rkgp", query_all, key_all, preferred_element_type=jnp.float32
    ) * HD ** (-0.5)
    valid_mask = ((offset + jnp.arange(positions, dtype=jnp.int32))[None, :] < length[:, None])[
        :, None, None, :
    ]
    masked = jnp.where(valid_mask, scores, neg_big)
    row_top = jnp.max(masked, axis=-1)
    weights = jnp.where(valid_mask, jnp.exp(masked - row_top[..., None]), 0.0).astype(jnp.bfloat16)
    row_total = jnp.sum(weights.astype(jnp.float32), axis=-1)
    mixed_sum = jnp.einsum(
        "rkgp,rpkd->rkgd", weights, value_all, preferred_element_type=jnp.float32
    )
    return (
        row_top.reshape(req_count, HQ),
        row_total.reshape(req_count, HQ),
        mixed_sum.reshape(req_count, HQ, HD),
    )


def on_device(
    hidden_rows,
    entering_rows,
    norm_gain,
    key_weight,
    value_weight,
    queries,
    cache_keys,
    cache_values,
    lengths,
    plan,
):
    tensor_size = lax.axis_size("tensor")
    tensor_rank = lax.axis_index("tensor")
    section_rank = lax.axis_index("section")
    slot_count = queries.shape[1]
    positions = cache_keys.shape[3]
    own_heads = HQ // tensor_size
    offset = tensor_rank * positions
    gain_row = norm_gain[0].astype(jnp.float32)
    head_ids = tensor_rank * own_heads + jnp.arange(own_heads, dtype=jnp.int32)
    select = (head_ids[:, None] // (HQ // KVH) == jnp.arange(KVH, dtype=jnp.int32)[None, :]).astype(
        jnp.float32
    )

    def slot_stats(slot_index):
        return cache_stats(
            queries[0, slot_index],
            cache_keys[0, slot_index],
            cache_values[0, slot_index],
            lengths[slot_index],
            offset,
        )

    def combine(stats):
        lead_count = stats[0].shape[0]
        req_count = stats[0].shape[1]
        row_top, row_total, mixed_sum = merged(stats, "tensor", join_parts)
        row_top = lax.dynamic_slice_in_dim(row_top, tensor_rank * own_heads, own_heads, 2)
        row_total = lax.dynamic_slice_in_dim(row_total, tensor_rank * own_heads, own_heads, 2)
        mixed_sum = lax.dynamic_slice_in_dim(
            mixed_sum, tensor_rank * own_heads, own_heads, 2
        ).reshape(lead_count, req_count, own_heads * HD)
        return (row_top, row_total, mixed_sum)

    state_rows = hidden_rows[0]
    req_count = state_rows.shape[0]
    for tick_index in range(slot_count):
        slot_now = plan[(section_rank - tick_index) % slot_count]
        row_top, row_total, mixed_sum = tuple(
            (
                element[0]
                for element in combine(
                    jax.tree.map(lambda element: element[None], slot_stats(slot_now))
                )
            )
        )
        length_now = lengths[slot_now]
        wide_rows = state_rows.astype(jnp.float32)
        scaled = (wide_rows * gain_row).astype(jnp.bfloat16)
        square, key_part, value_part = lax.psum(
            (
                jnp.sum(wide_rows * wide_rows, axis=1),
                jnp.dot(scaled, key_weight[0], preferred_element_type=jnp.float32),
                jnp.dot(scaled, value_weight[0], preferred_element_type=jnp.float32),
            ),
            "tensor",
        )
        inverse = lax.rsqrt(square / D + epsilon)[:, None]
        new_key = rounded(rotate_keys((key_part * inverse).reshape(req_count, KVH, HD), length_now))
        new_value = rounded((value_part * inverse).reshape(req_count, KVH, HD))
        key_for = jnp.einsum("hk,rkd->rhd", select, new_key, precision=lax.Precision.HIGHEST)
        value_for = jnp.einsum("hk,rkd->rhd", select, new_value, precision=lax.Precision.HIGHEST)
        query_own = lax.dynamic_slice_in_dim(
            queries[0, slot_now].reshape(req_count, HQ, HD), tensor_rank * own_heads, own_heads, 1
        ).astype(jnp.float32)
        own_score = jnp.sum(query_own * key_for, axis=-1) * HD ** (-0.5)
        new_top = jnp.maximum(row_top, own_score)
        shrink = jnp.exp(row_top - new_top)
        own_weight = jnp.exp(own_score - new_top)
        row_total = row_total * shrink + own_weight
        mixed_sum = (
            mixed_sum.reshape(req_count, own_heads, HD) * shrink[..., None]
            + own_weight[..., None] * value_for
        )
        attention = (mixed_sum / row_total[..., None]).reshape(req_count, own_heads * HD)
        state_rows = (wide_rows + attention).astype(jnp.bfloat16)
        if tick_index + 1 < slot_count:
            moved_rows = from_behind(state_rows, "section", 1)
            state_rows = jnp.where(section_rank == 0, entering_rows[tick_index], moved_rows)
    return state_rows[None]


def solution(mesh):
    in_specs = (
        P("section", None, "tensor"),
        P(None, None, "tensor"),
        P("section", "tensor"),
        P("section", "tensor", None),
        P("section", "tensor", None),
        P("section", None, None, None),
        P("section", None, None, "tensor", None),
        P("section", None, None, "tensor", None),
        P(),
        P(),
    )
    out_specs = P("section", None, "tensor")
    return jax.shard_map(
        on_device, mesh=mesh, in_specs=in_specs, out_specs=out_specs, check_vma=False
    )
```

profile of v0, /device:TPU:449, one launch (start us, length us, event | category | flops | bytes accessed | tf_op | source)
XLA Modules:
  0.0 348.3 jit_solution(13550455425604246394)
XLA Ops:
  0.0 1.5 fusion.169
  6.6 0.6 and_select_fusion
  9.7 1.0 fusion.128
  10.8 0.5 copy-done.15
  11.4 0.7 mul.924
  12.1 0.8 fusion.78
  12.9 1.2 fusion.62
  14.1 0.9 fusion.70
  15.0 25.1 %all-reduce.3 = (f32[2,512]{1,0:T(2,128)S(1)}, f32[2]{0:T(128)S(1)}, f32[2,512]{1,0:T(2,128)S(1)}) all-reduce(f32[2,512]{1,0:T(2,128)S(1)} %fusion.62, f32[2]{0:T(128)S(1)} %fusion.78, f32[2,512]{1,0:T(2,128)S(1)} %fusion.70), channel_id=1, replica_groups=mesh['section'=32,'tensor'=16] {'tensor'}, use_global_device_ids=true, to_apply=%region_8.9 | all-reduce | flops 2050 | bytes 16400 | tf_op jit(solution)/shard_map/psum | solution.py:156
  40.2 0.7 multiply_cosine_fusion
  41.0 0.7 pad_maximum_fusion
  41.8 2.1 constant_dynamic-slice_fusion.12
  43.9 1.1 copy.51
  45.0 0.6 copy-done.12
  46.4 0.3 convolution_convert_fusion.3
  46.7 18.6 %all_gather.50 = bf16[16,1,2,64,128]{4,3,2,1,0:T(8,128)(2,1)S(1)} all-gather(bf16[1,1,2,64,128]{4,3,2,1,0:T(8,128)(2,1)S(1)} %bitcast.476), channel_id=1, replica_groups=mesh['section'=32,'tensor'=16] {'tensor'}, dimensions={0}, use_global_device_ids=true | all-gather | bytes 557056 | tf_op jit(solution)/shard_map/all_gather | solution.py:18
  65.3 15.8 %all_gather.49 = bf16[16,1,2,64]{3,2,1,0:T(2,128)(2,1)S(1)} all-gather(bf16[1,1,2,64]{3,2,1,0:T(2,128)(2,1)S(1)} %convert_element_type.741), channel_id=1, replica_groups=mesh['section'=32,'tensor'=16] {'tensor'}, dimensions={0}, use_global_device_ids=true | all-gather | bytes 4352 | tf_op jit(solution)/shard_map/all_gather | solution.py:18
  81.2 14.3 %all_gather.48 = bf16[16,1,2,64]{3,2,1,0:T(2,128)(2,1)S(1)} all-gather(bf16[1,1,2,64]{3,2,1,0:T(2,128)(2,1)S(1)} %convert_element_type.737), channel_id=1, replica_groups=mesh['section'=32,'tensor'=16] {'tensor'}, dimensions={0}, use_global_device_ids=true | all-gather | bytes 4352 | tf_op jit(solution)/shard_map/all_gather | solution.py:18
  95.5 2.9 while.76
  98.5 0.7 copy-done.10
  99.1 0.3 fusion.52
  99.7 0.5 copy-done.4
  100.2 3.1 collective-permute-start
  104.1 0.3 convolution_convert_fusion.2
  104.4 17.6 %all_gather.53 = bf16[16,1,2,64,128]{4,3,2,1,0:T(8,128)(2,1)S(1)} all-gather(bf16[1,1,2,64,128]{4,3,2,1,0:T(8,128)(2,1)S(1)} %bitcast.477), channel_id=1, replica_groups=mesh['section'=32,'tensor'=16] {'tensor'}, dimensions={0}, use_global_device_ids=true | all-gather | bytes 557056 | tf_op jit(solution)/shard_map/all_gather | solution.py:18
  122.1 14.3 %all_gather.52 = bf16[16,1,2,64]{3,2,1,0:T(2,128)(2,1)S(1)} all-gather(bf16[1,1,2,64]{3,2,1,0:T(2,128)(2,1)S(1)} %convert_element_type.762), channel_id=1, replica_groups=mesh['section'=32,'tensor'=16] {'tensor'}, dimensions={0}, use_global_device_ids=true | all-gather | bytes 4352 | tf_op jit(solution)/shard_map/all_gather | solution.py:18
  136.5 15.7 %all_gather.51 = bf16[16,1,2,64]{3,2,1,0:T(2,128)(2,1)S(1)} all-gather(bf16[1,1,2,64]{3,2,1,0:T(2,128)(2,1)S(1)} %convert_element_type.758), channel_id=1, replica_groups=mesh['section'=32,'tensor'=16] {'tensor'}, dimensions={0}, use_global_device_ids=true | all-gather | bytes 4352 | tf_op jit(solution)/shard_map/all_gather | solution.py:18
  152.2 2.9 while.77
  155.9 0.3 convolution_convert_fusion.1
  156.2 16.0 %all_gather.56 = bf16[16,1,2,64,128]{4,3,2,1,0:T(8,128)(2,1)S(1)} all-gather(bf16[1,1,2,64,128]{4,3,2,1,0:T(8,128)(2,1)S(1)} %bitcast.478), channel_id=1, replica_groups=mesh['section'=32,'tensor'=16] {'tensor'}, dimensions={0}, use_global_device_ids=true | all-gather | bytes 557056 | tf_op jit(solution)/shard_map/all_gather | solution.py:18
  172.2 15.6 %all_gather.55 = bf16[16,1,2,64]{3,2,1,0:T(2,128)(2,1)S(1)} all-gather(bf16[1,1,2,64]{3,2,1,0:T(2,128)(2,1)S(1)} %convert_element_type.781), channel_id=1, replica_groups=mesh['section'=32,'tensor'=16] {'tensor'}, dimensions={0}, use_global_device_ids=true | all-gather | bytes 4352 | tf_op jit(solution)/shard_map/all_gather | solution.py:18
  187.9 14.3 %all_gather.54 = bf16[16,1,2,64]{3,2,1,0:T(2,128)(2,1)S(1)} all-gather(bf16[1,1,2,64]{3,2,1,0:T(2,128)(2,1)S(1)} %convert_element_type.777), channel_id=1, replica_groups=mesh['section'=32,'tensor'=16] {'tensor'}, dimensions={0}, use_global_device_ids=true | all-gather | bytes 4352 | tf_op jit(solution)/shard_map/all_gather | solution.py:18
  202.3 2.9 while.78
  206.0 0.3 convolution_convert_fusion
  206.3 17.4 %all_gather.59 = bf16[16,1,2,64,128]{4,3,2,1,0:T(8,128)(2,1)S(1)} all-gather(bf16[1,1,2,64,128]{4,3,2,1,0:T(8,128)(2,1)S(1)} %bitcast.479), channel_id=1, replica_groups=mesh['section'=32,'tensor'=16] {'tensor'}, dimensions={0}, use_global_device_ids=true | all-gather | bytes 557056 | tf_op jit(solution)/shard_map/all_gather | solution.py:18
  223.8 14.3 %all_gather.58 = bf16[16,1,2,64]{3,2,1,0:T(2,128)(2,1)S(1)} all-gather(bf16[1,1,2,64]{3,2,1,0:T(2,128)(2,1)S(1)} %convert_element_type.800), channel_id=1, replica_groups=mesh['section'=32,'tensor'=16] {'tensor'}, dimensions={0}, use_global_device_ids=true | all-gather | bytes 4352 | tf_op jit(solution)/shard_map/all_gather | solution.py:18
  238.2 15.7 %all_gather.57 = bf16[16,1,2,64]{3,2,1,0:T(2,128)(2,1)S(1)} all-gather(bf16[1,1,2,64]{3,2,1,0:T(2,128)(2,1)S(1)} %convert_element_type.796), channel_id=1, replica_groups=mesh['section'=32,'tensor'=16] {'tensor'}, dimensions={0}, use_global_device_ids=true | all-gather | bytes 4352 | tf_op jit(solution)/shard_map/all_gather | solution.py:18
  254.4 24.0 %all-reduce.2 = (f32[2,512]{1,0:T(2,128)S(1)}, f32[2]{0:T(128)S(1)}, f32[2,512]{1,0:T(2,128)S(1)}) all-reduce(f32[2,512]{1,0:T(2,128)S(1)} %fusion.60, f32[2]{0:T(128)S(1)} %get-tuple-element.822, f32[2,512]{1,0:T(2,128)S(1)} %fusion.68), channel_id=1, replica_groups=mesh['section'=32,'tensor'=16] {'tensor'}, use_global_device_ids=true, to_apply=%region_17.18 | all-reduce | flops 2050 | bytes 16400 | tf_op jit(solution)/shard_map/psum | solution.py:156
  278.5 0.7 copy-done.8
  279.9 3.1 collective-permute-start.1
  283.0 3.3 collective-permute-done.1
  286.8 26.0 %all-reduce.1 = (f32[2,512]{1,0:T(2,128)S(1)}, f32[2]{0:T(128)S(1)}, f32[2,512]{1,0:T(2,128)S(1)}) all-reduce(f32[2,512]{1,0:T(2,128)S(1)} %fusion.58, f32[2]{0:T(128)S(1)} %get-tuple-element.817, f32[2,512]{1,0:T(2,128)S(1)} %fusion.66), channel_id=1, replica_groups=mesh['section'=32,'tensor'=16] {'tensor'}, use_global_device_ids=true, to_apply=%region_26.27 | all-reduce | flops 2050 | bytes 16400 | tf_op jit(solution)/shard_map/psum | solution.py:156
  312.9 0.7 copy-done.6
  314.3 1.9 collective-permute-start.2
  316.2 2.9 while.79
  319.1 1.6 collective-permute-done.2
  321.2 25.7 %all-reduce = (f32[2,512]{1,0:T(2,128)S(1)}, f32[2]{0:T(128)S(1)}, f32[2,512]{1,0:T(2,128)S(1)}) all-reduce(f32[2,512]{1,0:T(2,128)S(1)} %fusion.56, f32[2]{0:T(128)S(1)} %get-tuple-element.812, f32[2,512]{1,0:T(2,128)S(1)} %fusion.64), channel_id=1, replica_groups=mesh['section'=32,'tensor'=16] {'tensor'}, use_global_device_ids=true, to_apply=%region_35.36 | all-reduce | flops 2050 | bytes 16400 | tf_op jit(solution)/shard_map/psum | solution.py:156
  347.7 0.6 fusion.102
  (370 shorter events, 17.6 us)
Async XLA Ops:
  0.0 14.1 %copy-start = (bf16[1,512,512]{2,1,0:T(8,128)(2,1)S(1)}, bf16[1,512,512]{2,1,0:T(8,128)(2,1)}, u32[]{:S(2)}) copy-start(bf16[1,512,512]{2,1,0:T(8,128)(2,1)} %param.21) | copy-start | bytes 1572868
  0.0 41.8 %copy-start.2 = (bf16[1,4,2,128,512]{4,3,2,1,0:T(8,128)(2,1)S(1)}, bf16[1,4,2,128,512]{4,3,2,1,0:T(8,128)(2,1)}, u32[]{:S(2)}) copy-start(bf16[1,4,2,128,512]{4,3,2,1,0:T(8,128)(2,1)} %param.25) | copy-start | bytes 3145732
  10.8 0.5 copy-start.15
  10.8 0.5 copy-start.13
  10.8 0.5 copy-start.17
  10.8 0.6 copy-start.11
  14.1 27.6 %copy-start.3 = (bf16[1,4,2,8192]{3,2,1,0:T(2,128)(2,1)S(1)}, bf16[1,4,2,8192]{3,2,1,0:T(2,128)(2,1)}, u32[]{:S(2)}) copy-start(bf16[1,4,2,8192]{3,2,1,0:T(2,128)(2,1)} %param.23) | copy-start | bytes 393220
  43.9 1.2 copy-start.18
  45.0 0.7 copy-start.12
  45.0 0.7 copy-start.14
  45.0 0.7 copy-start.16
  98.4 0.7 copy-start.10
  98.4 0.7 copy-start.19
  99.5 0.7 copy-start.4
  100.2 153.7 %collective-permute-start = (bf16[2,512]{1,0:T(2,128)(2,1)S(1)}, bf16[2,512]{1,0:T(2,128)(2,1)S(1)}, u32[]{:S(2)}, u32[]{:S(2)}) collective-permute-start(bf16[2,512]{1,0:T(2,128)(2,1)S(1)} %fusion.79), channel_id=1, source_target_pairs={{0,16},{16,32},{32,48},{48,64},{64,80},{80,96},{96,112},{112,128},... | collective-permute-start | bytes 6152 | tf_op jit(solution)/shard_map/ppermute | solution.py:34
  206.3 47.9 %copy-start.1 = (bf16[1,512,512]{2,1,0:T(8,128)(2,1)S(1)}, bf16[1,512,512]{2,1,0:T(8,128)(2,1)}, u32[]{:S(2)}) copy-start(bf16[1,512,512]{2,1,0:T(8,128)(2,1)} %param.22) | copy-start | bytes 1572868
  238.1 15.8 %copy-start.5 = (bf16[3,2,512]{2,1,0:T(2,128)(2,1)S(1)}, bf16[3,2,512]{2,1,0:T(2,128)(2,1)}, u32[]{:S(2)}) copy-start(bf16[3,2,512]{2,1,0:T(2,128)(2,1)} %param.19) | copy-start | bytes 18436
  254.2 24.3 %copy-start.9 = (f32[2,64]{1,0:T(2,128)S(1)}, f32[2,64]{1,0:T(2,128)}, u32[]{:S(2)}) copy-start(f32[2,64]{1,0:T(2,128)} %get-tuple-element.872) | copy-start | bytes 1540
  278.5 0.7 copy-start.8
  279.9 6.4 %collective-permute-start.1 = (bf16[2,512]{1,0:T(2,128)(2,1)S(1)}, bf16[2,512]{1,0:T(2,128)(2,1)S(1)}, u32[]{:S(2)}, u32[]{:S(2)}) collective-permute-start(bf16[2,512]{1,0:T(2,128)(2,1)S(1)} %fusion.83), channel_id=1, source_target_pairs={{0,16},{16,32},{32,48},{48,64},{64,80},{80,96},{96,112},{112,128},... | collective-permute-start | bytes 6152 | tf_op jit(solution)/shard_map/ppermute | solution.py:34
  286.6 26.3 %copy-start.7 = (f32[2,64]{1,0:T(2,128)S(1)}, f32[2,64]{1,0:T(2,128)}, u32[]{:S(2)}) copy-start(f32[2,64]{1,0:T(2,128)} %get-tuple-element.874) | copy-start | bytes 1540
  312.9 0.7 copy-start.6
  314.3 6.4 %collective-permute-start.2 = (bf16[2,512]{1,0:T(2,128)(2,1)S(1)}, bf16[2,512]{1,0:T(2,128)(2,1)S(1)}, u32[]{:S(2)}, u32[]{:S(2)}) collective-permute-start(bf16[2,512]{1,0:T(2,128)(2,1)S(1)} %fusion.86), channel_id=1, source_target_pairs={{0,16},{16,32},{32,48},{48,64},{64,80},{80,96},{96,112},{112,128},... | collective-permute-start | bytes 6152 | tf_op jit(solution)/shard_map/ppermute | solution.py:34
where the time goes:
time: 351 us; the launch traced here: 348 us
  blocking collectives  290 us (83%)
  other arithmetic  15.6 us (4%)
  local copies, waits for them, and re-layouts  11.7 us (3%)
  starting transfers between devices  8.15 us (2%)
  between operations  8.01 us (2%)
  matrix products  7.15 us (2%)
  waiting for transfers between devices  4.89 us (1%)
    all_gather x12, blocking collectives, merged(): lax.all_gather(part.astype(kind), axis)  190 us
    psum x4, blocking collectives, on_device(): lax.psum((jnp.sum(wide_rows * wide_rows, axis=1), jnp.dot(scaled, key_wei...  101 us
    ppermute x3, starting transfers between devices, from_behind(): return lax.ppermute(block, axis, route)  8.15 us
  transfers between devices with their start and end apart: 3, of which 2 were waited for; matrix products, arithmetic and copies ran while one was open for 3% of the time, Pallas kernels for 0%

commit v1 on v0

v1 whole, which is shorter than its diff:
```python
import functools

import jax
import jax.numpy as jnp
from jax import lax
from jax.experimental import pallas as pl
from jax.experimental.pallas import tpu as pltpu
from jax.sharding import PartitionSpec as P

D = 8192
HQ = 64
KVH = 4
HD = 128
TICKS = 4
TENSOR = 16
EPSILON = 1e-05
NEG_BIG = -1e30
MESH = pl.DeviceIdType.MESH
f32 = jnp.float32
bf16 = jnp.bfloat16


def iota(shape, axis):
    return lax.broadcasted_iota(jnp.int32, shape, axis)


def block_diagonal(columns):
    group = iota((HD, HD), 1) // 32
    return jnp.concatenate(
        [jnp.where(group == k, columns, 0.0) for k in range(KVH)], axis=0
    ).astype(bf16)


def kernel(
    hidden_ref,
    entering_ref,
    gain_ref,
    kw_hbm,
    vw_hbm,
    q_hbm,
    ck_hbm,
    cv_hbm,
    len_ref,
    plan_ref,
    out_ref,
    kw,
    vw,
    qv,
    ck,
    cv,
    qs,
    folded,
    part_out,
    part_in,
    stat_out,
    stat_in,
    row_out,
    row_in,
    load_sem,
    part_send,
    part_recv,
    stat_send,
    stat_recv,
    row_send,
    row_recv,
):
    sections = lax.axis_size("section")
    sec = lax.axis_index("section")
    ten = lax.axis_index("tensor")
    following = lax.rem(sec + 1, sections)
    previous = lax.rem(sec + sections - 1, sections)

    loads = [
        pltpu.make_async_copy(src, dst, load_sem.at[i])
        for i, (src, dst) in enumerate(
            [
                (q_hbm.at[0], qv),
                (kw_hbm.at[0], kw),
                (vw_hbm.at[0], vw),
                (ck_hbm.at[0], ck),
                (cv_hbm.at[0], cv),
            ]
        )
    ]
    for load in loads:
        load.start()

    barrier = pltpu.get_barrier_semaphore()
    for k in range(TENSOR):
        pl.semaphore_signal(barrier, inc=1, device_id=(previous, k), device_id_type=MESH)

    slots = [plan_ref[lax.rem(sec + TICKS - j, TICKS)] for j in range(TICKS)]
    spans = [[len_ref[r, slots[j]] for r in range(2)] for j in range(TICKS)]

    row8 = iota((8, HD), 0)
    lane8 = iota((8, HD), 1)
    even_row = row8 % 2 == 0
    lane1 = iota((1, HD), 1)
    even_lane = lane1 % 2 == 0
    mine = lane8 == row8 + ten * 8

    def heads_of(block):
        return jnp.concatenate([block[:, h * HD : (h + 1) * HD] for h in range(4)], axis=0)

    def features_of(block):
        return jnp.concatenate([block[2 * h : 2 * h + 2, :] for h in range(4)], axis=1)

    gain2 = jnp.broadcast_to(gain_ref[...].astype(f32), (2, 512))
    gain8 = heads_of(gain2)

    angle_rows = jnp.zeros((8, HD), f32)
    for j in range(TICKS):
        for r in range(2):
            angle_rows = jnp.where(row8 == 2 * j + r, spans[j][r].astype(f32), angle_rows)
    rates = jnp.exp((lane8 % 64).astype(f32) * (-2.0 * jnp.log(f32(500000.0)) / HD))
    angle = angle_rows * rates
    cosines = jnp.cos(angle)
    sines = jnp.sin(angle)
    sines = jnp.where(lane8 < 64, sines, -sines)

    def query_columns(j):
        rows = qv[slots[j]].astype(f32)
        for h in range(HQ):
            qs[2 * h : 2 * h + 2, :] = rows[:, h * HD : (h + 1) * HD]
        q = qs[...]
        cos8 = jnp.concatenate([cosines[2 * j : 2 * j + 2]] * 4, axis=0)
        sin8 = jnp.concatenate([sines[2 * j : 2 * j + 2]] * 4, axis=0)
        other = pltpu.roll(q, 64, 1)
        turned = (
            q.reshape(16, 8, HD) * cos8[None] + other.reshape(16, 8, HD) * sin8[None]
        ).reshape(HD, HD)
        return block_diagonal(q.T), block_diagonal(turned.T)

    def fold(j, turned):
        folded[j] = jnp.dot(kw[...], turned, preferred_element_type=f32).astype(bf16)

    def stats(j, columns):
        keys = ck[slots[j]].reshape(256, 512)
        both = jnp.dot(keys, columns, preferred_element_type=f32)
        scores = jnp.where(even_lane, both[:HD], both[HD:]) * HD ** (-0.5)
        span = jnp.where(even_lane, spans[j][0], spans[j][1])
        valid = iota((HD, HD), 0) + ten * HD < span
        scores = jnp.where(valid, scores, NEG_BIG)
        top = jnp.max(scores, axis=0, keepdims=True).astype(bf16).astype(f32)
        weights = jnp.where(valid, jnp.exp(scores - top), 0.0).astype(bf16).astype(f32)
        total = jnp.sum(weights, axis=0, keepdims=True)
        turned = weights.T
        even = iota((HD, HD), 0) % 2 == 0
        wide = jnp.concatenate(
            [jnp.where(even, turned, 0.0), jnp.where(even, 0.0, turned)], axis=1
        ).astype(bf16)
        values = cv[slots[j]].reshape(256, 512)
        high = total.astype(bf16).astype(f32)
        extra = jnp.where(
            row8 == 0, top, jnp.where(row8 == 1, high, jnp.where(row8 == 2, total - high, 0.0))
        )
        for k in range(KVH):
            mixed = jnp.dot(
                wide[32 * k : 32 * k + 32],
                values[:, HD * k : HD * k + HD],
                preferred_element_type=f32,
            )
            for i in range(4):
                stat_out[j, 4 * k + i] = jnp.concatenate(
                    [mixed[8 * i : 8 * i + 8], extra], axis=0
                ).astype(bf16)
        if j < TICKS - 1:
            for k in range(TENSOR):
                to = lax.rem(ten + k, TENSOR)
                pltpu.make_async_remote_copy(
                    stat_out.at[j, to],
                    stat_in.at[j, ten],
                    stat_send.at[j],
                    stat_recv.at[j],
                    device_id=(following, to),
                    device_id_type=MESH,
                ).start()
        else:
            for k in range(1, TENSOR):
                to = lax.rem(ten + k, TENSOR)
                pltpu.make_async_remote_copy(
                    stat_out.at[j, to],
                    stat_in.at[j, ten],
                    stat_send.at[j],
                    stat_recv.at[j],
                    device_id=(sec, to),
                    device_id_type=MESH,
                ).start()
            stat_in[j, ten] = stat_out[j, ten]

    def wait_bytes(ref, sem):
        pltpu.make_async_copy(ref, ref, sem).wait()

    def arrived(ref, j):
        return ref.at[j] if j < TICKS - 1 else ref.at[j, pl.ds(0, TENSOR - 1)]

    def merge(j):
        wait_bytes(arrived(stat_in, j), stat_recv.at[j])
        pages = stat_in[j].astype(f32)
        mixed = pages[:, 0:8, :]
        tops = pages[:, 8:9, :]
        totals = pages[:, 9:10, :] + pages[:, 10:11, :]
        top = jnp.max(tops, axis=0, keepdims=True)
        scale = jnp.exp(tops - top)
        total = jnp.sum(scale * totals, axis=0, keepdims=True)
        share = scale / total
        column = jnp.sum(jnp.where(mine[None], share, 0.0), axis=2, keepdims=True)
        mean = jnp.sum(column * mixed, axis=0)
        return mean, (top + jnp.log(total))[0]

    def combine(j, rows, merged):
        mean, level = merged
        wait_bytes(arrived(part_in, j), part_recv.at[j])
        sums = jnp.sum(part_in[j], axis=0)
        mean_sq = sums[3:4] / D + EPSILON
        own = sums[2:3] * lax.rsqrt(mean_sq * HD)
        share = 1.0 / (1.0 + jnp.exp(level - own))
        inverse = lax.rsqrt(mean_sq)
        share_col = jnp.sum(jnp.where(mine, share, 0.0), axis=1, keepdims=True)
        inverse_col = jnp.sum(jnp.where(mine, inverse, 0.0), axis=1, keepdims=True)
        fresh = jnp.where(even_row, sums[0:1], sums[1:2]) * inverse_col
        return (rows + (mean + share_col * (fresh - mean))).astype(bf16).astype(f32)

    def project(j, rows):
        scaled = features_of(rows * gain8).astype(bf16)
        value_part = jnp.dot(scaled, vw[...], preferred_element_type=f32)
        own_part = jnp.dot(scaled, folded[j], preferred_element_type=f32)
        own_row = jnp.where(even_lane, own_part[0:1], own_part[1:2])
        square = rows * rows
        square = square[0:2] + square[2:4] + square[4:6] + square[6:8]
        square = jnp.sum(square, axis=1, keepdims=True)
        square_row = jnp.where(even_lane, square[0:1], square[1:2])
        tail = jnp.concatenate([own_row, square_row], axis=0)
        for k in range(KVH):
            part_out[j, k] = jnp.concatenate(
                [value_part[:, HD * k : HD * k + HD], tail], axis=0
            )

    def send_parts(j):
        for k in range(TENSOR):
            if j == TICKS - 1 and k == 0:
                continue
            to = lax.rem(ten + k, TENSOR)
            pltpu.make_async_remote_copy(
                part_out.at[j, to // 4],
                part_in.at[j, ten],
                part_send.at[j],
                part_recv.at[j],
                device_id=(following if j < TICKS - 1 else sec, to),
                device_id_type=MESH,
            ).start()
        if j == TICKS - 1:
            part_in[j, ten] = part_out[j, ten // 4]

    def row_copy(j):
        return pltpu.make_async_remote_copy(
            row_out.at[j],
            row_in.at[j],
            row_send.at[j],
            row_recv.at[j],
            device_id=(following, ten),
            device_id_type=MESH,
        )

    def send_rows(j, rows):
        row_out[j] = rows
        row_copy(j).start()

    rows = heads_of(hidden_ref[0].astype(f32))
    loads[0].wait()
    columns, turned = query_columns(0)
    loads[1].wait()
    fold(0, turned)
    loads[2].wait()
    project(0, rows)
    pl.semaphore_wait(barrier, TENSOR)
    send_parts(0)
    send_rows(0, rows)
    loads[3].wait()
    loads[4].wait()
    stats(0, columns)
    columns, turned = query_columns(1)
    fold(1, turned)
    stats(1, columns)
    for j in range(1, TICKS):
        row_copy(j - 1).wait_recv()
        merged = merge(j - 1)
        fresh = combine(j - 1, row_in[j - 1], merged)
        rows = jnp.where(sec == 0, heads_of(entering_ref[j - 1].astype(f32)), fresh)
        project(j, rows)
        send_parts(j)
        if j < TICKS - 1:
            send_rows(j, rows)
            columns, turned = query_columns(j + 1)
            fold(j + 1, turned)
            stats(j + 1, columns)
    merged = merge(TICKS - 1)
    final = combine(TICKS - 1, rows, merged)
    out_ref[0] = features_of(final).astype(bf16)

    for j in range(TICKS):
        wait_bytes(arrived(part_in, j), part_send.at[j])
        wait_bytes(arrived(stat_in, j), stat_send.at[j])
        if j < TICKS - 1:
            row_copy(j).wait_send()


def on_device(
    hidden_rows,
    entering_rows,
    norm_gain,
    key_weight,
    value_weight,
    queries,
    cache_keys,
    cache_values,
    lengths,
    plan,
):
    vmem = pl.BlockSpec(memory_space=pltpu.VMEM)
    smem = pl.BlockSpec(memory_space=pltpu.SMEM)
    anywhere = pl.BlockSpec(memory_space=pl.ANY)
    dma = pltpu.SemaphoreType.DMA
    return pl.pallas_call(
        kernel,
        out_shape=jax.ShapeDtypeStruct((1, 2, 512), bf16),
        in_specs=[vmem, vmem, vmem] + [anywhere] * 5 + [smem, smem],
        out_specs=vmem,
        scratch_shapes=[
            pltpu.VMEM((512, 512), bf16),
            pltpu.VMEM((512, 512), bf16),
            pltpu.VMEM((4, 2, 8192), bf16),
            pltpu.VMEM((4, 2, 128, 512), bf16),
            pltpu.VMEM((4, 2, 128, 512), bf16),
            pltpu.VMEM((128, 128), f32),
            pltpu.VMEM((TICKS, 512, 128), bf16),
            pltpu.VMEM((TICKS, KVH, 4, 128), f32),
            pltpu.VMEM((TICKS, TENSOR, 4, 128), f32),
            pltpu.VMEM((TICKS, TENSOR, 16, 128), bf16),
            pltpu.VMEM((TICKS, TENSOR, 16, 128), bf16),
            pltpu.VMEM((TICKS - 1, 8, 128), f32),
            pltpu.VMEM((TICKS - 1, 8, 128), f32),
            dma((5,)),
            dma((TICKS,)),
            dma((TICKS,)),
            dma((TICKS,)),
            dma((TICKS,)),
            dma((TICKS - 1,)),
            dma((TICKS - 1,)),
        ],
        compiler_params=pltpu.CompilerParams(
            collective_id=0, has_side_effects=True, vmem_limit_bytes=60 * 1024 * 1024
        ),
    )(
        hidden_rows,
        entering_rows,
        norm_gain,
        key_weight,
        value_weight,
        queries,
        cache_keys,
        cache_values,
        lengths.T,
        plan,
    )


def solution(mesh):
    in_specs = (
        P("section", None, "tensor"),
        P(None, None, "tensor"),
        P("section", "tensor"),
        P("section", "tensor", None),
        P("section", "tensor", None),
        P("section", None, None, None),
        P("section", None, None, "tensor", None),
        P("section", None, None, "tensor", None),
        P(),
        P(),
    )
    out_specs = P("section", None, "tensor")
    return jax.shard_map(
        on_device, mesh=mesh, in_specs=in_specs, out_specs=out_specs, check_vma=False
    )
```

time: 351 us -> 44.3 us (0.13)
  the two profiles are of different devices: /device:TPU:449 before, /device:TPU:1 now
where the time goes in v1:
time: 44.3 us; the launch traced here: 44.1 us
  Pallas kernels  42.8 us (97%)
  local copies, waits for them, and re-layouts  1.26 us (3%)
    pallas_call x1, Pallas kernels, on_device(): pl.pallas_call(kernel, out_shape=jax.ShapeDtypeStruct((1, 2, 512), bf16),...  42.8 us
    unnamed x1, local copies, waits for them, and re-layouts  1.26 us

profile of v1, /device:TPU:1, one launch (start us, length us, event | category | flops | bytes accessed | tf_op | source)
XLA Modules:
  0.0 44.1 jit_solution(14297071357216910493)
XLA Ops:
  0.0 42.8 %shard_map.100 = bf16[1,2,512]{2,1,0:T(2,128)(2,1)} custom-call(bf16[1,2,512]{2,1,0:T(2,128)(2,1)} %hidden_ref.1, bf16[3,2,512]{2,1,0:T(2,128)(2,1)} %entering_ref.1, bf16[1,512]{1,0:T(2,128)(2,1)} %gain_ref.1, bf16[1,512,512]{2,1,0:T(8,128)(2,1)} %kw_hbm.1, bf16[1,512,512]{2,1,0:T(8,128)(2,1)} %vw_hbm.1, bf16[1,4,2,8192]{3,2,1,0:T(2,128)(2,1)} %q_hbm.1, ...), custom_call_target="tpu_custom_call" | custom-call | tf_op jit(solution)/shard_map/pallas_call | solution.py:324
  42.8 1.3 %copy.12 = bf16[1,2,512]{2,1,0:T(2,128)(2,1)} copy(bf16[1,2,512]{2,1,0:T(2,128)(2,1)} %shard_map.100) | data formatting | bytes 4096

commit v2 on v1

--- a/solution.py
+++ b/solution.py
@@ -32,17 +32,22 @@
 
 
 def kernel(
-    hidden_ref,
-    entering_ref,
-    gain_ref,
+    hidden_hbm,
+    entering_hbm,
+    gain_hbm,
     kw_hbm,
     vw_hbm,
     q_hbm,
     ck_hbm,
     cv_hbm,
+    len_hbm,
+    plan_hbm,
+    out_ref,
     len_ref,
     plan_ref,
-    out_ref,
+    hidden_ref,
+    entering_ref,
+    gain_ref,
     kw,
     vw,
     qv,
@@ -70,25 +75,44 @@
     following = lax.rem(sec + 1, sections)
     previous = lax.rem(sec + sections - 1, sections)
 
-    loads = [
-        pltpu.make_async_copy(src, dst, load_sem.at[i])
-        for i, (src, dst) in enumerate(
-            [
-                (q_hbm.at[0], qv),
-                (kw_hbm.at[0], kw),
-                (vw_hbm.at[0], vw),
-                (ck_hbm.at[0], ck),
-                (cv_hbm.at[0], cv),
-            ]
-        )
-    ]
-    for load in loads:
-        load.start()
+    load = {}
+    for i, (name, src, dst) in enumerate(
+        [
+            ("plan", plan_hbm, plan_ref),
+            ("len", len_hbm, len_ref),
+            ("q", q_hbm.at[0], qv),
+            ("hidden", hidden_hbm.at[0], hidden_ref),
+            ("gain", gain_hbm, gain_ref),
+            ("kw", kw_hbm.at[0], kw),
+            ("ck", ck_hbm.at[0], ck),
+            ("vw", vw_hbm.at[0], vw),
+            ("cv", cv_hbm.at[0], cv),
+            ("entering", entering_hbm, entering_ref),
+        ]
+    ):
+        load[name] = pltpu.make_async_copy(src, dst, load_sem.at[i])
+        load[name].start()
+
+    first = sec == 0
+    last = sec == sections - 1
+    chip = ten // 2 * 2
+    partner = chip + 1 - lax.rem(ten, 2)
+    others = [lax.rem(chip + m, TENSOR) for m in (8, 9, 6, 7, 10, 11, 4, 5, 12, 13, 2, 3, 14, 15)]
 
     barrier = pltpu.get_barrier_semaphore()
-    for k in range(TENSOR):
-        pl.semaphore_signal(barrier, inc=1, device_id=(previous, k), device_id_type=MESH)
-
+
+    @pl.when(jnp.logical_not(first))
+    def _():
+        for k in others + [partner, ten]:
+            pl.semaphore_signal(barrier, inc=1, device_id=(previous, k), device_id_type=MESH)
+
+    @pl.when(first)
+    def _():
+        for k in others + [partner]:
+            pl.semaphore_signal(barrier, inc=1, device_id=(sec, k), device_id_type=MESH)
+
+    load["plan"].wait()
+    load["len"].wait()
     slots = [plan_ref[lax.rem(sec + TICKS - j, TICKS)] for j in range(TICKS)]
     spans = [[len_ref[r, slots[j]] for r in range(2)] for j in range(TICKS)]
 
@@ -104,9 +128,6 @@
 
     def features_of(block):
         return jnp.concatenate([block[2 * h : 2 * h + 2, :] for h in range(4)], axis=1)
-
-    gain2 = jnp.broadcast_to(gain_ref[...].astype(f32), (2, 512))
-    gain8 = heads_of(gain2)
 
     angle_rows = jnp.zeros((8, HD), f32)
     for j in range(TICKS):
@@ -164,28 +185,30 @@
                 stat_out[j, 4 * k + i] = jnp.concatenate(
                     [mixed[8 * i : 8 * i + 8], extra], axis=0
                 ).astype(bf16)
-        if j < TICKS - 1:
-            for k in range(TENSOR):
-                to = lax.rem(ten + k, TENSOR)
+
+    def send_page(source, target, j, send, receive):
+        def to_section(section, partners):
+            for to in partners:
                 pltpu.make_async_remote_copy(
-                    stat_out.at[j, to],
-                    stat_in.at[j, ten],
-                    stat_send.at[j],
-                    stat_recv.at[j],
-                    device_id=(following, to),
+                    source(to),
+                    target.at[j, ten],
+                    send.at[j],
+                    receive.at[j],
+                    device_id=(section, to),
                     device_id_type=MESH,
                 ).start()
+
+        if j < TICKS - 1:
+
+            @pl.when(jnp.logical_not(last))
+            def _():
+                to_section(following, others + [partner, ten])
         else:
-            for k in range(1, TENSOR):
-                to = lax.rem(ten + k, TENSOR)
-                pltpu.make_async_remote_copy(
-                    stat_out.at[j, to],
-                    stat_in.at[j, ten],
-                    stat_send.at[j],
-                    stat_recv.at[j],
-                    device_id=(sec, to),
-                    device_id_type=MESH,
-                ).start()
+            to_section(sec, others + [partner])
+
+    def send_stats(j):
+        send_page(lambda to: stat_out.at[j, to], stat_in, j, stat_send, stat_recv)
+        if j == TICKS - 1:
             stat_in[j, ten] = stat_out[j, ten]
 
     def wait_bytes(ref, sem):
@@ -221,10 +244,15 @@
         fresh = jnp.where(even_row, sums[0:1], sums[1:2]) * inverse_col
         return (rows + (mean + share_col * (fresh - mean))).astype(bf16).astype(f32)
 
-    def project(j, rows):
+    def project(j, rows, turned=None):
         scaled = features_of(rows * gain8).astype(bf16)
+        if turned is None:
+            own_part = jnp.dot(scaled, folded[j], preferred_element_type=f32)
+        else:
+            key_part = jnp.dot(scaled, kw[...], preferred_element_type=f32).astype(bf16)
+            own_part = jnp.dot(key_part, turned, preferred_element_type=f32)
+        load_wait("vw", j == 0)
         value_part = jnp.dot(scaled, vw[...], preferred_element_type=f32)
-        own_part = jnp.dot(scaled, folded[j], preferred_element_type=f32)
         own_row = jnp.where(even_lane, own_part[0:1], own_part[1:2])
         square = rows * rows
         square = square[0:2] + square[2:4] + square[4:6] + square[6:8]
@@ -236,19 +264,12 @@
                 [value_part[:, HD * k : HD * k + HD], tail], axis=0
             )
 
+    def load_wait(name, wanted=True):
+        if wanted:
+            load[name].wait()
+
     def send_parts(j):
-        for k in range(TENSOR):
-            if j == TICKS - 1 and k == 0:
-                continue
-            to = lax.rem(ten + k, TENSOR)
-            pltpu.make_async_remote_copy(
-                part_out.at[j, to // 4],
-                part_in.at[j, ten],
-                part_send.at[j],
-                part_recv.at[j],
-                device_id=(following if j < TICKS - 1 else sec, to),
-                device_id_type=MESH,
-            ).start()
+        send_page(lambda to: part_out.at[j, to // 4], part_in, j, part_send, part_recv)
         if j == TICKS - 1:
             part_in[j, ten] = part_out[j, ten // 4]
 
@@ -262,47 +283,74 @@
             device_id_type=MESH,
         )
 
-    def send_rows(j, rows):
-        row_out[j] = rows
-        row_copy(j).start()
-
-    rows = heads_of(hidden_ref[0].astype(f32))
-    loads[0].wait()
+    def send_rows(j):
+        @pl.when(jnp.logical_not(last))
+        def _():
+            row_copy(j).start()
+
+    load["q"].wait()
     columns, turned = query_columns(0)
-    loads[1].wait()
-    fold(0, turned)
-    loads[2].wait()
-    project(0, rows)
-    pl.semaphore_wait(barrier, TENSOR)
+    load["hidden"].wait()
+    load["gain"].wait()
+    gain8 = heads_of(jnp.broadcast_to(gain_ref[...].astype(f32), (2, 512)))
+    rows = heads_of(hidden_ref[...].astype(f32))
+    row_out[0] = rows
+    load["kw"].wait()
+    project(0, rows, turned)
+    load["ck"].wait()
+    load["cv"].wait()
+    stats(0, columns)
+    load["entering"].wait()
+
+    @pl.when(first)
+    def _():
+        pl.semaphore_wait(barrier, 2 * TENSOR - 1)
+
+    @pl.when(jnp.logical_not(jnp.logical_or(first, last)))
+    def _():
+        pl.semaphore_wait(barrier, TENSOR)
+
     send_parts(0)
-    send_rows(0, rows)
-    loads[3].wait()
-    loads[4].wait()
-    stats(0, columns)
+    send_stats(0)
+    send_rows(0)
     columns, turned = query_columns(1)
     fold(1, turned)
     stats(1, columns)
+    send_stats(1)
     for j in range(1, TICKS):
-        row_copy(j - 1).wait_recv()
-        merged = merge(j - 1)
-        fresh = combine(j - 1, row_in[j - 1], merged)
-        rows = jnp.where(sec == 0, heads_of(entering_ref[j - 1].astype(f32)), fresh)
+
+        @pl.when(first)
+        def _():
+            row_out[j] = heads_of(entering_ref[j - 1].astype(f32))
+
+        @pl.when(jnp.logical_not(first))
+        def _():
+            row_copy(j - 1).wait_recv()
+            merged = merge(j - 1)
+            row_out[j] = combine(j - 1, row_in[j - 1], merged)
+
+        rows = row_out[j]
         project(j, rows)
         send_parts(j)
         if j < TICKS - 1:
-            send_rows(j, rows)
+            send_rows(j)
             columns, turned = query_columns(j + 1)
             fold(j + 1, turned)
             stats(j + 1, columns)
+            send_stats(j + 1)
     merged = merge(TICKS - 1)
     final = combine(TICKS - 1, rows, merged)
     out_ref[0] = features_of(final).astype(bf16)
 
-    for j in range(TICKS):
-        wait_bytes(arrived(part_in, j), part_send.at[j])
-        wait_bytes(arrived(stat_in, j), stat_send.at[j])
-        if j < TICKS - 1:
+    @pl.when(jnp.logical_not(last))
+    def _():
+        for j in range(TICKS - 1):
+            wait_bytes(part_in.at[j], part_send.at[j])
+            wait_bytes(stat_in.at[j], stat_send.at[j])
             row_copy(j).wait_send()
+
+    wait_bytes(arrived(part_in, TICKS - 1), part_send.at[TICKS - 1])
+    wait_bytes(arrived(stat_in, TICKS - 1), stat_send.at[TICKS - 1])
 
 
 def on_device(
@@ -318,15 +366,19 @@
     plan,
 ):
     vmem = pl.BlockSpec(memory_space=pltpu.VMEM)
-    smem = pl.BlockSpec(memory_space=pltpu.SMEM)
     anywhere = pl.BlockSpec(memory_space=pl.ANY)
     dma = pltpu.SemaphoreType.DMA
     return pl.pallas_call(
         kernel,
         out_shape=jax.ShapeDtypeStruct((1, 2, 512), bf16),
-        in_specs=[vmem, vmem, vmem] + [anywhere] * 5 + [smem, smem],
+        in_specs=[anywhere] * 10,
         out_specs=vmem,
         scratch_shapes=[
+            pltpu.SMEM((2, 4), jnp.int32),
+            pltpu.SMEM((4,), jnp.int32),
+            pltpu.VMEM((2, 512), bf16),
+            pltpu.VMEM((3, 2, 512), bf16),
+            pltpu.VMEM((1, 512), bf16),
             pltpu.VMEM((512, 512), bf16),
             pltpu.VMEM((512, 512), bf16),
             pltpu.VMEM((4, 2, 8192), bf16),
@@ -338,9 +390,9 @@
             pltpu.VMEM((TICKS, TENSOR, 4, 128), f32),
             pltpu.VMEM((TICKS, TENSOR, 16, 128), bf16),
             pltpu.VMEM((TICKS, TENSOR, 16, 128), bf16),
+            pltpu.VMEM((TICKS, 8, 128), f32),
             pltpu.VMEM((TICKS - 1, 8, 128), f32),
-            pltpu.VMEM((TICKS - 1, 8, 128), f32),
-            dma((5,)),
+            dma((10,)),
             dma((TICKS,)),
             dma((TICKS,)),
             dma((TICKS,)),

time: 44.3 us -> 33.6 us (0.76)
  the two profiles are of different devices: /device:TPU:1 before, /device:TPU:261 now
where the time goes in v2:
time: 33.6 us; the launch traced here: 33.4 us
  Pallas kernels  32.1 us (96%)
  local copies, waits for them, and re-layouts  1.26 us (4%)
    pallas_call x1, Pallas kernels, on_device(): pl.pallas_call(kernel, out_shape=jax.ShapeDtypeStruct((1, 2, 512), bf16),...  32.1 us
    unnamed x1, local copies, waits for them, and re-layouts  1.26 us

profile of v2, /device:TPU:261, one launch (start us, length us, event | category | flops | bytes accessed | tf_op | source)
XLA Modules:
  0.0 33.4 jit_solution(1370915905703558461)
XLA Ops:
  0.0 32.1 %shard_map.100 = bf16[1,2,512]{2,1,0:T(2,128)(2,1)} custom-call(bf16[1,2,512]{2,1,0:T(2,128)(2,1)} %hidden_hbm.1, bf16[3,2,512]{2,1,0:T(2,128)(2,1)} %entering_hbm.1, bf16[1,512]{1,0:T(2,128)(2,1)} %gain_hbm.1, bf16[1,512,512]{2,1,0:T(8,128)(2,1)} %kw_hbm.1, bf16[1,512,512]{2,1,0:T(8,128)(2,1)} %vw_hbm.1, bf16[1,4,2,8192]{3,2,1,0:T(2,128)(2,1)} %q_hbm.1, ...), custom_call_target="tpu_custom_call" | custom-call | tf_op jit(solution)/shard_map/pallas_call | solution.py:371
  32.1 1.3 %copy.12 = bf16[1,2,512]{2,1,0:T(2,128)(2,1)} copy(bf16[1,2,512]{2,1,0:T(2,128)(2,1)} %shard_map.100) | data formatting | bytes 4096

commit v3 on v2

--- a/solution.py
+++ b/solution.py
@@ -59,6 +59,7 @@
     part_in,
     stat_out,
     stat_in,
+    mixed_in,
     row_out,
     row_in,
     load_sem,
@@ -74,6 +75,24 @@
     ten = lax.axis_index("tensor")
     following = lax.rem(sec + 1, sections)
     previous = lax.rem(sec + sections - 1, sections)
+
+    first = sec == 0
+    last = sec == sections - 1
+    chip = ten // 2 * 2
+    partner = chip + 1 - lax.rem(ten, 2)
+    others = [lax.rem(chip + m, TENSOR) for m in (8, 9, 6, 7, 10, 11, 4, 5, 12, 13, 2, 3, 14, 15)]
+
+    barrier = pltpu.get_barrier_semaphore()
+
+    @pl.when(jnp.logical_not(first))
+    def _():
+        for k in others + [partner, ten]:
+            pl.semaphore_signal(barrier, inc=1, device_id=(previous, k), device_id_type=MESH)
+
+    @pl.when(first)
+    def _():
+        for k in others + [partner]:
+            pl.semaphore_signal(barrier, inc=1, device_id=(sec, k), device_id_type=MESH)
 
     load = {}
     for i, (name, src, dst) in enumerate(
@@ -93,24 +112,6 @@
         load[name] = pltpu.make_async_copy(src, dst, load_sem.at[i])
         load[name].start()
 
-    first = sec == 0
-    last = sec == sections - 1
-    chip = ten // 2 * 2
-    partner = chip + 1 - lax.rem(ten, 2)
-    others = [lax.rem(chip + m, TENSOR) for m in (8, 9, 6, 7, 10, 11, 4, 5, 12, 13, 2, 3, 14, 15)]
-
-    barrier = pltpu.get_barrier_semaphore()
-
-    @pl.when(jnp.logical_not(first))
-    def _():
-        for k in others + [partner, ten]:
-            pl.semaphore_signal(barrier, inc=1, device_id=(previous, k), device_id_type=MESH)
-
-    @pl.when(first)
-    def _():
-        for k in others + [partner]:
-            pl.semaphore_signal(barrier, inc=1, device_id=(sec, k), device_id_type=MESH)
-
     load["plan"].wait()
     load["len"].wait()
     slots = [plan_ref[lax.rem(sec + TICKS - j, TICKS)] for j in range(TICKS)]
@@ -122,6 +123,7 @@
     lane1 = iota((1, HD), 1)
     even_lane = lane1 % 2 == 0
     mine = lane8 == row8 + ten * 8
+    mine_square = lane8 == lax.rem(row8 + ten * 8 + 64, HD)
 
     def heads_of(block):
         return jnp.concatenate([block[:, h * HD : (h + 1) * HD] for h in range(4)], axis=0)
@@ -171,10 +173,7 @@
             [jnp.where(even, turned, 0.0), jnp.where(even, 0.0, turned)], axis=1
         ).astype(bf16)
         values = cv[slots[j]].reshape(256, 512)
-        high = total.astype(bf16).astype(f32)
-        extra = jnp.where(
-            row8 == 0, top, jnp.where(row8 == 1, high, jnp.where(row8 == 2, total - high, 0.0))
-        )
+        level = jnp.concatenate([top, total], axis=0).astype(bf16)
         for k in range(KVH):
             mixed = jnp.dot(
                 wide[32 * k : 32 * k + 32],
@@ -182,9 +181,10 @@
                 preferred_element_type=f32,
             )
             for i in range(4):
-                stat_out[j, 4 * k + i] = jnp.concatenate(
-                    [mixed[8 * i : 8 * i + 8], extra], axis=0
-                ).astype(bf16)
+                for p in range(4):
+                    at = 8 * i + 2 * p
+                    stat_out[j, 4 * k + i, p] = mixed[at : at + 2].astype(bf16)
+                stat_out[j, 4 * k + i, 4] = level
 
     def send_page(source, target, j, send, receive):
         def to_section(section, partners):
@@ -219,30 +219,33 @@
 
     def merge(j):
         wait_bytes(arrived(stat_in, j), stat_recv.at[j])
-        pages = stat_in[j].astype(f32)
-        mixed = pages[:, 0:8, :]
-        tops = pages[:, 8:9, :]
-        totals = pages[:, 9:10, :] + pages[:, 10:11, :]
+        for k in range(TENSOR):
+            for p in range(4):
+                mixed_in[k, 2 * p : 2 * p + 2] = stat_in[j, k, p].astype(f32)
+        mixed = mixed_in[...]
+        levels = stat_in[j, :, 4].astype(f32)
+        tops = levels[:, 0:1, :]
+        totals = levels[:, 1:2, :]
         top = jnp.max(tops, axis=0, keepdims=True)
         scale = jnp.exp(tops - top)
         total = jnp.sum(scale * totals, axis=0, keepdims=True)
         share = scale / total
         column = jnp.sum(jnp.where(mine[None], share, 0.0), axis=2, keepdims=True)
         mean = jnp.sum(column * mixed, axis=0)
-        return mean, (top + jnp.log(total))[0]
+        level = (top + jnp.log(total))[0]
+        return mean, jnp.sum(jnp.where(mine, level, 0.0), axis=1, keepdims=True)
 
     def combine(j, rows, merged):
         mean, level = merged
         wait_bytes(arrived(part_in, j), part_recv.at[j])
-        sums = jnp.sum(part_in[j], axis=0)
-        mean_sq = sums[3:4] / D + EPSILON
-        own = sums[2:3] * lax.rsqrt(mean_sq * HD)
-        share = 1.0 / (1.0 + jnp.exp(level - own))
-        inverse = lax.rsqrt(mean_sq)
-        share_col = jnp.sum(jnp.where(mine, share, 0.0), axis=1, keepdims=True)
-        inverse_col = jnp.sum(jnp.where(mine, inverse, 0.0), axis=1, keepdims=True)
-        fresh = jnp.where(even_row, sums[0:1], sums[1:2]) * inverse_col
-        return (rows + (mean + share_col * (fresh - mean))).astype(bf16).astype(f32)
+        sums = jnp.sum(part_in[j].astype(f32), axis=0)
+        mixture = sums[2:3] + sums[3:4]
+        own_col = jnp.sum(jnp.where(mine, mixture, 0.0), axis=1, keepdims=True)
+        square_col = jnp.sum(jnp.where(mine_square, mixture, 0.0), axis=1, keepdims=True)
+        inverse = lax.rsqrt(square_col / D + EPSILON)
+        share = 1.0 / (1.0 + jnp.exp(level - own_col * inverse * HD ** (-0.5)))
+        fresh = jnp.where(even_row, sums[0:1], sums[1:2]) * inverse
+        return (rows + (mean + share * (fresh - mean))).astype(bf16).astype(f32)
 
     def project(j, rows, turned=None):
         scaled = features_of(rows * gain8).astype(bf16)
@@ -258,11 +261,12 @@
         square = square[0:2] + square[2:4] + square[4:6] + square[6:8]
         square = jnp.sum(square, axis=1, keepdims=True)
         square_row = jnp.where(even_lane, square[0:1], square[1:2])
-        tail = jnp.concatenate([own_row, square_row], axis=0)
         for k in range(KVH):
+            mixture = jnp.where(lane1 // 32 == k, own_row, square_row)
+            high = mixture.astype(bf16).astype(f32)
             part_out[j, k] = jnp.concatenate(
-                [value_part[:, HD * k : HD * k + HD], tail], axis=0
-            )
+                [value_part[:, HD * k : HD * k + HD], high, mixture - high], axis=0
+            ).astype(bf16)
 
     def load_wait(name, wanted=True):
         if wanted:
@@ -370,7 +374,7 @@
     dma = pltpu.SemaphoreType.DMA
     return pl.pallas_call(
         kernel,
-        out_shape=jax.ShapeDtypeStruct((1, 2, 512), bf16),
+        out_shape=pltpu.VMEM((1, 2, 512), bf16),
         in_specs=[anywhere] * 10,
         out_specs=vmem,
         scratch_shapes=[
@@ -386,10 +390,11 @@
             pltpu.VMEM((4, 2, 128, 512), bf16),
             pltpu.VMEM((128, 128), f32),
             pltpu.VMEM((TICKS, 512, 128), bf16),
-            pltpu.VMEM((TICKS, KVH, 4, 128), f32),
-            pltpu.VMEM((TICKS, TENSOR, 4, 128), f32),
-            pltpu.VMEM((TICKS, TENSOR, 16, 128), bf16),
-            pltpu.VMEM((TICKS, TENSOR, 16, 128), bf16),
+            pltpu.VMEM((TICKS, KVH, 4, 128), bf16),
+            pltpu.VMEM((TICKS, TENSOR, 4, 128), bf16),
+            pltpu.VMEM((TICKS, TENSOR, 5, 2, 128), bf16),
+            pltpu.VMEM((TICKS, TENSOR, 5, 2, 128), bf16),
+            pltpu.VMEM((TENSOR, 8, 128), f32),
             pltpu.VMEM((TICKS, 8, 128), f32),
             pltpu.VMEM((TICKS - 1, 8, 128), f32),
             dma((10,)),

time: 33.6 us -> 31.7 us (0.943)
  Pallas kernels: 32.1 us -> 31 us
  local copies, waits for them, and re-layouts: 1.26 us -> 0.58 us
    pallas_call x1, Pallas kernels: 32.1 us -> 31 us  [on_device(): pl.pallas_call(kernel, out_shape=pltpu.VMEM((1, 2, 512), bf16), in_specs=...]
    unnamed x1, local copies, waits for them, and re-layouts: 1.26 us -> 0.58 us
where the time goes in v3:
time: 31.7 us; the launch traced here: 31.6 us
  Pallas kernels  31 us (98%)
  local copies, waits for them, and re-layouts  0.58 us (2%)
    pallas_call x1, Pallas kernels, on_device(): pl.pallas_call(kernel, out_shape=pltpu.VMEM((1, 2, 512), bf16), in_specs=...  31 us

profile of v3, /device:TPU:261, one launch (start us, length us, event | category | flops | bytes accessed | tf_op | source)
XLA Modules:
  0.0 31.6 jit_solution(7961331513548759950)
XLA Ops:
  0.0 31.0 %shard_map.100 = bf16[1,2,512]{2,1,0:T(2,128)(2,1)S(1)} custom-call(bf16[1,2,512]{2,1,0:T(2,128)(2,1)} %hidden_hbm.1, bf16[3,2,512]{2,1,0:T(2,128)(2,1)} %entering_hbm.1, bf16[1,512]{1,0:T(2,128)(2,1)} %gain_hbm.1, bf16[1,512,512]{2,1,0:T(8,128)(2,1)} %kw_hbm.1, bf16[1,512,512]{2,1,0:T(8,128)(2,1)} %vw_hbm.1, bf16[1,4,2,8192]{3,2,1,0:T(2,128)(2,1)} %q_hbm.1, ...), custom_call_target="tpu_custom_call" | custom-call | tf_op jit(solution)/shard_map/pallas_call | solution.py:375
  31.0 0.6 %copy.12 = bf16[1,2,512]{2,1,0:T(2,128)(2,1)} copy(bf16[1,2,512]{2,1,0:T(2,128)(2,1)S(1)} %shard_map.100) | data formatting | bytes 4096

commit v4 on v3

--- a/solution.py
+++ b/solution.py
@@ -186,17 +186,18 @@
                     stat_out[j, 4 * k + i, p] = mixed[at : at + 2].astype(bf16)
                 stat_out[j, 4 * k + i, 4] = level
 
-    def send_page(source, target, j, send, receive):
+    def send_pages(j, kinds):
         def to_section(section, partners):
             for to in partners:
-                pltpu.make_async_remote_copy(
-                    source(to),
-                    target.at[j, ten],
-                    send.at[j],
-                    receive.at[j],
-                    device_id=(section, to),
-                    device_id_type=MESH,
-                ).start()
+                for source, target, send, receive in kinds:
+                    pltpu.make_async_remote_copy(
+                        source(to),
+                        target.at[j, ten],
+                        send.at[j],
+                        receive.at[j],
+                        device_id=(section, to),
+                        device_id_type=MESH,
+                    ).start()
 
         if j < TICKS - 1:
 
@@ -206,10 +207,21 @@
         else:
             to_section(sec, others + [partner])
 
+    def stat_pages(j):
+        return (lambda to: stat_out.at[j, to], stat_in, stat_send, stat_recv)
+
+    def part_pages(j):
+        return (lambda to: part_out.at[j, to // 4], part_in, part_send, part_recv)
+
     def send_stats(j):
-        send_page(lambda to: stat_out.at[j, to], stat_in, j, stat_send, stat_recv)
+        send_pages(j, [stat_pages(j)])
         if j == TICKS - 1:
             stat_in[j, ten] = stat_out[j, ten]
+
+    def send_parts(j):
+        send_pages(j, [part_pages(j)])
+        if j == TICKS - 1:
+            part_in[j, ten] = part_out[j, ten // 4]
 
     def wait_bytes(ref, sem):
         pltpu.make_async_copy(ref, ref, sem).wait()
@@ -235,8 +247,7 @@
         level = (top + jnp.log(total))[0]
         return mean, jnp.sum(jnp.where(mine, level, 0.0), axis=1, keepdims=True)
 
-    def combine(j, rows, merged):
-        mean, level = merged
+    def arrival(j, level):
         wait_bytes(arrived(part_in, j), part_recv.at[j])
         sums = jnp.sum(part_in[j].astype(f32), axis=0)
         mixture = sums[2:3] + sums[3:4]
@@ -244,8 +255,7 @@
         square_col = jnp.sum(jnp.where(mine_square, mixture, 0.0), axis=1, keepdims=True)
         inverse = lax.rsqrt(square_col / D + EPSILON)
         share = 1.0 / (1.0 + jnp.exp(level - own_col * inverse * HD ** (-0.5)))
-        fresh = jnp.where(even_row, sums[0:1], sums[1:2]) * inverse
-        return (rows + (mean + share * (fresh - mean))).astype(bf16).astype(f32)
+        return share, inverse, jnp.where(even_row, sums[0:1], sums[1:2])
 
     def project(j, rows, turned=None):
         scaled = features_of(rows * gain8).astype(bf16)
@@ -256,26 +266,63 @@
             own_part = jnp.dot(key_part, turned, preferred_element_type=f32)
         load_wait("vw", j == 0)
         value_part = jnp.dot(scaled, vw[...], preferred_element_type=f32)
-        own_row = jnp.where(even_lane, own_part[0:1], own_part[1:2])
         square = rows * rows
         square = square[0:2] + square[2:4] + square[4:6] + square[6:8]
         square = jnp.sum(square, axis=1, keepdims=True)
+        write_parts(j, value_part, own_part, square)
+
+    def write_parts(j, values, own, square):
+        own_row = jnp.where(even_lane, own[0:1], own[1:2])
         square_row = jnp.where(even_lane, square[0:1], square[1:2])
         for k in range(KVH):
             mixture = jnp.where(lane1 // 32 == k, own_row, square_row)
             high = mixture.astype(bf16).astype(f32)
             part_out[j, k] = jnp.concatenate(
-                [value_part[:, HD * k : HD * k + HD], high, mixture - high], axis=0
+                [values[0:2, HD * k : HD * k + HD], high, mixture - high], axis=0
             ).astype(bf16)
+
+    def blocks(rows):
+        return jnp.concatenate(
+            [jnp.where(row8 // 2 == h, rows, 0.0) for h in range(4)], axis=1
+        ).astype(bf16)
+
+    def over_heads(rows):
+        rows = rows + pltpu.roll(rows, 4, 0)
+        return rows + pltpu.roll(rows, 2, 0)
+
+    def dots(left, right):
+        return jnp.sum(left * right, axis=1, keepdims=True)
+
+    def advance(j):
+        row_copy(j - 1).wait_recv()
+        rows = row_in[j - 1]
+        mean, level = merge(j - 1)
+        known = jnp.concatenate([blocks(rows * gain8), blocks(mean * gain8)], axis=0)
+        known_value = jnp.dot(known, vw[...], preferred_element_type=f32)
+        known_own = jnp.dot(known, folded[j], preferred_element_type=f32)
+        rows_rows, rows_mean, mean_mean = dots(rows, rows), dots(rows, mean), dots(mean, mean)
+        share, inverse, fresh = arrival(j - 1, level)
+        scaled = blocks(fresh * gain8)
+        fresh_value = jnp.dot(scaled, vw[...], preferred_element_type=f32)
+        fresh_own = jnp.dot(scaled, folded[j], preferred_element_type=f32)
+        rest = 1.0 - share
+        factor = share * inverse
+        square = (
+            rows_rows
+            + rest * (2.0 * rows_mean + rest * mean_mean)
+            + factor * (2.0 * (dots(rows, fresh) + rest * dots(mean, fresh)) + factor * dots(fresh, fresh))
+        )
+        write_parts(
+            j,
+            over_heads(known_value[:8] + rest * known_value[8:] + factor * fresh_value),
+            over_heads(known_own[:8] + rest * known_own[8:] + factor * fresh_own),
+            over_heads(jnp.broadcast_to(square, (8, HD))),
+        )
+        row_out[j] = (rows + rest * mean + factor * fresh).astype(bf16).astype(f32)
 
     def load_wait(name, wanted=True):
         if wanted:
             load[name].wait()
-
-    def send_parts(j):
-        send_page(lambda to: part_out.at[j, to // 4], part_in, j, part_send, part_recv)
-        if j == TICKS - 1:
-            part_in[j, ten] = part_out[j, ten // 4]
 
     def row_copy(j):
         return pltpu.make_async_remote_copy(
@@ -314,8 +361,7 @@
     def _():
         pl.semaphore_wait(barrier, TENSOR)
 
-    send_parts(0)
-    send_stats(0)
+    send_pages(0, [part_pages(0), stat_pages(0)])
     send_rows(0)
     columns, turned = query_columns(1)
     fold(1, turned)
@@ -325,16 +371,14 @@
 
         @pl.when(first)
         def _():
-            row_out[j] = heads_of(entering_ref[j - 1].astype(f32))
+            rows = heads_of(entering_ref[j - 1].astype(f32))
+            row_out[j] = rows
+            project(j, rows)
 
         @pl.when(jnp.logical_not(first))
         def _():
-            row_copy(j - 1).wait_recv()
-            merged = merge(j - 1)
-            row_out[j] = combine(j - 1, row_in[j - 1], merged)
-
-        rows = row_out[j]
-        project(j, rows)
+            advance(j)
+
         send_parts(j)
         if j < TICKS - 1:
             send_rows(j)
@@ -342,8 +386,10 @@
             fold(j + 1, turned)
             stats(j + 1, columns)
             send_stats(j + 1)
-    merged = merge(TICKS - 1)
-    final = combine(TICKS - 1, rows, merged)
+    rows = row_out[TICKS - 1]
+    mean, level = merge(TICKS - 1)
+    share, inverse, fresh = arrival(TICKS - 1, level)
+    final = rows + (mean + share * (fresh * inverse - mean))
     out_ref[0] = features_of(final).astype(bf16)
 
     @pl.when(jnp.logical_not(last))

time: 31.7 us -> 31.3 us (0.987)
  Pallas kernels: 31 us -> 30.6 us
    pallas_call x1, Pallas kernels: 31 us -> 30.6 us  [on_device(): pl.pallas_call(kernel, out_shape=pltpu.VMEM((1, 2, 512), bf16), in_specs=...]
where the time goes in v4:
time: 31.3 us; the launch traced here: 31.2 us
  Pallas kernels  30.6 us (98%)
  local copies, waits for them, and re-layouts  0.58 us (2%)
    pallas_call x1, Pallas kernels, on_device(): pl.pallas_call(kernel, out_shape=pltpu.VMEM((1, 2, 512), bf16), in_specs=...  30.6 us

profile of v4, /device:TPU:261, one launch (start us, length us, event | category | flops | bytes accessed | tf_op | source)
XLA Modules:
  0.0 31.2 jit_solution(4238330463285980733)
XLA Ops:
  0.0 30.6 %shard_map.100 = bf16[1,2,512]{2,1,0:T(2,128)(2,1)S(1)} custom-call(bf16[1,2,512]{2,1,0:T(2,128)(2,1)} %hidden_hbm.1, bf16[3,2,512]{2,1,0:T(2,128)(2,1)} %entering_hbm.1, bf16[1,512]{1,0:T(2,128)(2,1)} %gain_hbm.1, bf16[1,512,512]{2,1,0:T(8,128)(2,1)} %kw_hbm.1, bf16[1,512,512]{2,1,0:T(8,128)(2,1)} %vw_hbm.1, bf16[1,4,2,8192]{3,2,1,0:T(2,128)(2,1)} %q_hbm.1, ...), custom_call_target="tpu_custom_call" | custom-call | tf_op jit(solution)/shard_map/pallas_call | solution.py:421
  30.6 0.6 %copy.12 = bf16[1,2,512]{2,1,0:T(2,128)(2,1)} copy(bf16[1,2,512]{2,1,0:T(2,128)(2,1)S(1)} %shard_map.100) | data formatting | bytes 4096

commit v5 on v4

--- a/solution.py
+++ b/solution.py
@@ -14,6 +14,8 @@
 TICKS = 4
 TENSOR = 16
 EPSILON = 1e-05
+SLOW_STEP = 15
+ALONE = TICKS
 NEG_BIG = -1e30
 MESH = pl.DeviceIdType.MESH
 f32 = jnp.float32
@@ -78,18 +80,24 @@
 
     first = sec == 0
     last = sec == sections - 1
+    alone = sec == SLOW_STEP
+    after = sec == SLOW_STEP + 1
     chip = ten // 2 * 2
     partner = chip + 1 - lax.rem(ten, 2)
     others = [lax.rem(chip + m, TENSOR) for m in (8, 9, 6, 7, 10, 11, 4, 5, 12, 13, 2, 3, 14, 15)]
 
     barrier = pltpu.get_barrier_semaphore()
 
-    @pl.when(jnp.logical_not(first))
+    @pl.when(jnp.logical_not(jnp.logical_or(first, after)))
     def _():
         for k in others + [partner, ten]:
             pl.semaphore_signal(barrier, inc=1, device_id=(previous, k), device_id_type=MESH)
 
-    @pl.when(first)
+    @pl.when(after)
+    def _():
+        pl.semaphore_signal(barrier, inc=1, device_id=(previous, ten), device_id_type=MESH)
+
+    @pl.when(jnp.logical_or(first, alone))
     def _():
         for k in others + [partner]:
             pl.semaphore_signal(barrier, inc=1, device_id=(sec, k), device_id_type=MESH)
@@ -186,26 +194,26 @@
                     stat_out[j, 4 * k + i, p] = mixed[at : at + 2].astype(bf16)
                 stat_out[j, 4 * k + i, 4] = level
 
+    def send_to(section, partners, kinds, slot):
+        for to in partners:
+            for source, target, send, receive in kinds:
+                pltpu.make_async_remote_copy(
+                    source(to),
+                    target.at[slot, ten],
+                    send.at[slot],
+                    receive.at[slot],
+                    device_id=(section, to),
+                    device_id_type=MESH,
+                ).start()
+
     def send_pages(j, kinds):
-        def to_section(section, partners):
-            for to in partners:
-                for source, target, send, receive in kinds:
-                    pltpu.make_async_remote_copy(
-                        source(to),
-                        target.at[j, ten],
-                        send.at[j],
-                        receive.at[j],
-                        device_id=(section, to),
-                        device_id_type=MESH,
-                    ).start()
-
         if j < TICKS - 1:
 
             @pl.when(jnp.logical_not(last))
             def _():
-                to_section(following, others + [partner, ten])
+                send_to(following, others + [partner, ten], kinds, j)
         else:
-            to_section(sec, others + [partner])
+            send_to(sec, others + [partner], kinds, j)
 
     def stat_pages(j):
         return (lambda to: stat_out.at[j, to], stat_in, stat_send, stat_recv)
@@ -256,6 +264,11 @@
         inverse = lax.rsqrt(square_col / D + EPSILON)
         share = 1.0 / (1.0 + jnp.exp(level - own_col * inverse * HD ** (-0.5)))
         return share, inverse, jnp.where(even_row, sums[0:1], sums[1:2])
+
+    def finish(slot, rows):
+        mean, level = merge(slot)
+        share, inverse, fresh = arrival(slot, level)
+        return rows + (mean + share * (fresh * inverse - mean))
 
     def project(j, rows, turned=None):
         scaled = features_of(rows * gain8).astype(bf16)
@@ -361,11 +374,28 @@
     def _():
         pl.semaphore_wait(barrier, TENSOR)
 
-    send_pages(0, [part_pages(0), stat_pages(0)])
-    send_rows(0)
+    kinds = [part_pages(0), stat_pages(0)]
+
+    @pl.when(jnp.logical_not(jnp.logical_or(last, alone)))
+    def _():
+        send_to(following, others + [partner, ten], kinds, 0)
+        row_copy(0).start()
+
+    @pl.when(alone)
+    def _():
+        send_to(sec, others + [partner], kinds, ALONE)
+        part_in[ALONE, ten] = part_out[0, ten // 4]
+        stat_in[ALONE, ten] = stat_out[0, ten]
+
     columns, turned = query_columns(1)
     fold(1, turned)
     stats(1, columns)
+
+    @pl.when(alone)
+    def _():
+        row_out[0] = finish(ALONE, row_out[0]).astype(bf16).astype(f32)
+        row_copy(0).start()
+
     send_stats(1)
     for j in range(1, TICKS):
 
@@ -375,9 +405,23 @@
             row_out[j] = rows
             project(j, rows)
 
-        @pl.when(jnp.logical_not(first))
-        def _():
-            advance(j)
+        if j == 1:
+
+            @pl.when(after)
+            def _():
+                row_copy(0).wait_recv()
+                rows = row_in[0]
+                row_out[1] = rows
+                project(1, rows)
+
+            @pl.when(jnp.logical_not(jnp.logical_or(first, after)))
+            def _():
+                advance(1)
+        else:
+
+            @pl.when(jnp.logical_not(first))
+            def _():
+                advance(j)
 
         send_parts(j)
         if j < TICKS - 1:
@@ -386,18 +430,26 @@
             fold(j + 1, turned)
             stats(j + 1, columns)
             send_stats(j + 1)
-    rows = row_out[TICKS - 1]
-    mean, level = merge(TICKS - 1)
-    share, inverse, fresh = arrival(TICKS - 1, level)
-    final = rows + (mean + share * (fresh * inverse - mean))
+    final = finish(TICKS - 1, row_out[TICKS - 1])
     out_ref[0] = features_of(final).astype(bf16)
 
     @pl.when(jnp.logical_not(last))
     def _():
         for j in range(TICKS - 1):
+            row_copy(j).wait_send()
+        for j in range(1, TICKS - 1):
             wait_bytes(part_in.at[j], part_send.at[j])
             wait_bytes(stat_in.at[j], stat_send.at[j])
-            row_copy(j).wait_send()
+
+    @pl.when(jnp.logical_not(jnp.logical_or(last, alone)))
+    def _():
+        wait_bytes(part_in.at[0], part_send.at[0])
+        wait_bytes(stat_in.at[0], stat_send.at[0])
+
+    @pl.when(alone)
+    def _():
+        wait_bytes(arrived(part_in, ALONE), part_send.at[ALONE])
+        wait_bytes(arrived(stat_in, ALONE), stat_send.at[ALONE])
 
     wait_bytes(arrived(part_in, TICKS - 1), part_send.at[TICKS - 1])
     wait_bytes(arrived(stat_in, TICKS - 1), stat_send.at[TICKS - 1])
@@ -437,17 +489,17 @@
             pltpu.VMEM((128, 128), f32),
             pltpu.VMEM((TICKS, 512, 128), bf16),
             pltpu.VMEM((TICKS, KVH, 4, 128), bf16),
-            pltpu.VMEM((TICKS, TENSOR, 4, 128), bf16),
+            pltpu.VMEM((TICKS + 1, TENSOR, 4, 128), bf16),
             pltpu.VMEM((TICKS, TENSOR, 5, 2, 128), bf16),
-            pltpu.VMEM((TICKS, TENSOR, 5, 2, 128), bf16),
+            pltpu.VMEM((TICKS + 1, TENSOR, 5, 2, 128), bf16),
             pltpu.VMEM((TENSOR, 8, 128), f32),
             pltpu.VMEM((TICKS, 8, 128), f32),
             pltpu.VMEM((TICKS - 1, 8, 128), f32),
             dma((10,)),
-            dma((TICKS,)),
-            dma((TICKS,)),
-            dma((TICKS,)),
-            dma((TICKS,)),
+            dma((TICKS + 1,)),
+            dma((TICKS + 1,)),
+            dma((TICKS + 1,)),
+            dma((TICKS + 1,)),
             dma((TICKS - 1,)),
             dma((TICKS - 1,)),
         ],

time: 31.3 us -> 30.7 us (0.981)
  the two profiles are of different devices: /device:TPU:261 before, /device:TPU:449 now
where the time goes in v5:
time: 30.7 us; the launch traced here: 30.6 us
  Pallas kernels  30 us (98%)
  local copies, waits for them, and re-layouts  0.58 us (2%)
    pallas_call x1, Pallas kernels, on_device(): pl.pallas_call(kernel, out_shape=pltpu.VMEM((1, 2, 512), bf16), in_specs=...  30 us

profile of v5, /device:TPU:449, one launch (start us, length us, event | category | flops | bytes accessed | tf_op | source)
XLA Modules:
  0.0 30.6 jit_solution(7403782263933313133)
XLA Ops:
  0.0 30.0 %shard_map.100 = bf16[1,2,512]{2,1,0:T(2,128)(2,1)S(1)} custom-call(bf16[1,2,512]{2,1,0:T(2,128)(2,1)} %hidden_hbm.1, bf16[3,2,512]{2,1,0:T(2,128)(2,1)} %entering_hbm.1, bf16[1,512]{1,0:T(2,128)(2,1)} %gain_hbm.1, bf16[1,512,512]{2,1,0:T(8,128)(2,1)} %kw_hbm.1, bf16[1,512,512]{2,1,0:T(8,128)(2,1)} %vw_hbm.1, bf16[1,4,2,8192]{3,2,1,0:T(2,128)(2,1)} %q_hbm.1, ...), custom_call_target="tpu_custom_call" | custom-call | tf_op jit(solution)/shard_map/pallas_call | solution.py:473
  30.0 0.6 %copy.12 = bf16[1,2,512]{2,1,0:T(2,128)(2,1)} copy(bf16[1,2,512]{2,1,0:T(2,128)(2,1)S(1)} %shard_map.100) | data formatting | bytes 4096

commit v6 on v5

--- a/solution.py
+++ b/solution.py
@@ -84,7 +84,7 @@
     after = sec == SLOW_STEP + 1
     chip = ten // 2 * 2
     partner = chip + 1 - lax.rem(ten, 2)
-    others = [lax.rem(chip + m, TENSOR) for m in (8, 9, 6, 7, 10, 11, 4, 5, 12, 13, 2, 3, 14, 15)]
+    others = [lax.rem(chip + m, TENSOR) for m in (8, 9, 10, 11, 6, 7, 12, 13, 4, 5, 14, 15, 2, 3)]
 
     barrier = pltpu.get_barrier_semaphore()
 
@@ -131,7 +131,7 @@
     lane1 = iota((1, HD), 1)
     even_lane = lane1 % 2 == 0
     mine = lane8 == row8 + ten * 8
-    mine_square = lane8 == lax.rem(row8 + ten * 8 + 64, HD)
+    mine_square = lane8 // 64 == 1 - ten // 8
 
     def heads_of(block):
         return jnp.concatenate([block[:, h * HD : (h + 1) * HD] for h in range(4)], axis=0)
@@ -260,7 +260,8 @@
         sums = jnp.sum(part_in[j].astype(f32), axis=0)
         mixture = sums[2:3] + sums[3:4]
         own_col = jnp.sum(jnp.where(mine, mixture, 0.0), axis=1, keepdims=True)
-        square_col = jnp.sum(jnp.where(mine_square, mixture, 0.0), axis=1, keepdims=True)
+        squares = jnp.where(even_row, sums[2:3], sums[3:4])
+        square_col = jnp.sum(jnp.where(mine_square, squares, 0.0), axis=1, keepdims=True)
         inverse = lax.rsqrt(square_col / D + EPSILON)
         share = 1.0 / (1.0 + jnp.exp(level - own_col * inverse * HD ** (-0.5)))
         return share, inverse, jnp.where(even_row, sums[0:1], sums[1:2])
@@ -279,19 +280,23 @@
             own_part = jnp.dot(key_part, turned, preferred_element_type=f32)
         load_wait("vw", j == 0)
         value_part = jnp.dot(scaled, vw[...], preferred_element_type=f32)
-        square = rows * rows
-        square = square[0:2] + square[2:4] + square[4:6] + square[6:8]
-        square = jnp.sum(square, axis=1, keepdims=True)
-        write_parts(j, value_part, own_part, square)
-
-    def write_parts(j, values, own, square):
+        write_parts(j, value_part, own_part, over_heads(rows * rows))
+
+    def write_parts(j, values, own, squares):
         own_row = jnp.where(even_lane, own[0:1], own[1:2])
-        square_row = jnp.where(even_lane, square[0:1], square[1:2])
+        high = own_row.astype(bf16).astype(f32)
+        low = own_row - high
+        squares = squares + pltpu.roll(squares, 64, 1)
         for k in range(KVH):
-            mixture = jnp.where(lane1 // 32 == k, own_row, square_row)
-            high = mixture.astype(bf16).astype(f32)
+            here = lane1 // 32 == k
+            there = lane1 // 64 == 1 - k // 2
             part_out[j, k] = jnp.concatenate(
-                [values[0:2, HD * k : HD * k + HD], high, mixture - high], axis=0
+                [
+                    values[0:2, HD * k : HD * k + HD],
+                    jnp.where(here, high, jnp.where(there, squares[0:1], 0.0)),
+                    jnp.where(here, low, jnp.where(there, squares[1:2], 0.0)),
+                ],
+                axis=0,
             ).astype(bf16)
 
     def blocks(rows):
@@ -302,9 +307,6 @@
     def over_heads(rows):
         rows = rows + pltpu.roll(rows, 4, 0)
         return rows + pltpu.roll(rows, 2, 0)
-
-    def dots(left, right):
-        return jnp.sum(left * right, axis=1, keepdims=True)
 
     def advance(j):
         row_copy(j - 1).wait_recv()
@@ -313,25 +315,20 @@
         known = jnp.concatenate([blocks(rows * gain8), blocks(mean * gain8)], axis=0)
         known_value = jnp.dot(known, vw[...], preferred_element_type=f32)
         known_own = jnp.dot(known, folded[j], preferred_element_type=f32)
-        rows_rows, rows_mean, mean_mean = dots(rows, rows), dots(rows, mean), dots(mean, mean)
         share, inverse, fresh = arrival(j - 1, level)
         scaled = blocks(fresh * gain8)
         fresh_value = jnp.dot(scaled, vw[...], preferred_element_type=f32)
         fresh_own = jnp.dot(scaled, folded[j], preferred_element_type=f32)
         rest = 1.0 - share
         factor = share * inverse
-        square = (
-            rows_rows
-            + rest * (2.0 * rows_mean + rest * mean_mean)
-            + factor * (2.0 * (dots(rows, fresh) + rest * dots(mean, fresh)) + factor * dots(fresh, fresh))
-        )
+        rows = rows + rest * mean + factor * fresh
         write_parts(
             j,
             over_heads(known_value[:8] + rest * known_value[8:] + factor * fresh_value),
             over_heads(known_own[:8] + rest * known_own[8:] + factor * fresh_own),
-            over_heads(jnp.broadcast_to(square, (8, HD))),
+            over_heads(rows * rows),
         )
-        row_out[j] = (rows + rest * mean + factor * fresh).astype(bf16).astype(f32)
+        row_out[j] = rows.astype(bf16).astype(f32)
 
     def load_wait(name, wanted=True):
         if wanted:

time: 30.7 us -> 30.7 us (level)
  no operation moved by 1% of the time
where the time goes in v6:
time: 30.7 us; the launch traced here: 30.5 us
  Pallas kernels  29.9 us (97%)
  local copies, waits for them, and re-layouts  0.58 us (2%)
    pallas_call x1, Pallas kernels, on_device(): pl.pallas_call(kernel, out_shape=pltpu.VMEM((1, 2, 512), bf16), in_specs=...  29.9 us

profile of v6, /device:TPU:449, one launch (start us, length us, event | category | flops | bytes accessed | tf_op | source)
XLA Modules:
  0.0 30.5 jit_solution(7983530062901178050)
XLA Ops:
  0.0 29.9 %shard_map.100 = bf16[1,2,512]{2,1,0:T(2,128)(2,1)S(1)} custom-call(bf16[1,2,512]{2,1,0:T(2,128)(2,1)} %hidden_hbm.1, bf16[3,2,512]{2,1,0:T(2,128)(2,1)} %entering_hbm.1, bf16[1,512]{1,0:T(2,128)(2,1)} %gain_hbm.1, bf16[1,512,512]{2,1,0:T(8,128)(2,1)} %kw_hbm.1, bf16[1,512,512]{2,1,0:T(8,128)(2,1)} %vw_hbm.1, bf16[1,4,2,8192]{3,2,1,0:T(2,128)(2,1)} %q_hbm.1, ...), custom_call_target="tpu_custom_call" | custom-call | tf_op jit(solution)/shard_map/pallas_call | solution.py:470
  29.9 0.6 %copy.12 = bf16[1,2,512]{2,1,0:T(2,128)(2,1)} copy(bf16[1,2,512]{2,1,0:T(2,128)(2,1)S(1)} %shard_map.100) | data formatting | bytes 4096

commit v7 on v5

--- a/solution.py
+++ b/solution.py
@@ -84,7 +84,7 @@
     after = sec == SLOW_STEP + 1
     chip = ten // 2 * 2
     partner = chip + 1 - lax.rem(ten, 2)
-    others = [lax.rem(chip + m, TENSOR) for m in (8, 9, 6, 7, 10, 11, 4, 5, 12, 13, 2, 3, 14, 15)]
+    others = [lax.rem(chip + m, TENSOR) for m in (8, 9, 10, 11, 6, 7, 12, 13, 4, 5, 14, 15, 2, 3)]
 
     barrier = pltpu.get_barrier_semaphore()
 

time: 30.7 us -> 30.7 us (level)
  no operation moved by 1% of the time
where the time goes in v7:
time: 30.7 us; the launch traced here: 30.5 us
  Pallas kernels  30 us (98%)
  local copies, waits for them, and re-layouts  0.58 us (2%)
    pallas_call x1, Pallas kernels, on_device(): pl.pallas_call(kernel, out_shape=pltpu.VMEM((1, 2, 512), bf16), in_specs=...  30 us

profile of v7, /device:TPU:449, one launch (start us, length us, event | category | flops | bytes accessed | tf_op | source)
XLA Modules:
  0.0 30.5 jit_solution(10289748399279334925)
XLA Ops:
  0.0 30.0 %shard_map.100 = bf16[1,2,512]{2,1,0:T(2,128)(2,1)S(1)} custom-call(bf16[1,2,512]{2,1,0:T(2,128)(2,1)} %hidden_hbm.1, bf16[3,2,512]{2,1,0:T(2,128)(2,1)} %entering_hbm.1, bf16[1,512]{1,0:T(2,128)(2,1)} %gain_hbm.1, bf16[1,512,512]{2,1,0:T(8,128)(2,1)} %kw_hbm.1, bf16[1,512,512]{2,1,0:T(8,128)(2,1)} %vw_hbm.1, bf16[1,4,2,8192]{3,2,1,0:T(2,128)(2,1)} %q_hbm.1, ...), custom_call_target="tpu_custom_call" | custom-call | tf_op jit(solution)/shard_map/pallas_call | solution.py:473
  30.0 0.6 %copy.12 = bf16[1,2,512]{2,1,0:T(2,128)(2,1)} copy(bf16[1,2,512]{2,1,0:T(2,128)(2,1)S(1)} %shard_map.100) | data formatting | bytes 4096
